TPU v7x, 32 devices: a whole 2x2x4 slice. The times are simulated.
32 devices in a mesh: stretch: 4 (over y, x), ctx: 8 (over z, core).
Axes of the slice: x: 2, y: 2, z: 4, core: 2. Of those that a mesh axis runs over, the one named last changes fastest.
Arguments:
- post_gate: bfloat16 [4096, 8192], P(('stretch', 'ctx')), may hold values from -6 to 6
- pre_gate: bfloat16 [4096, 8192], P(('stretch', 'ctx')), may hold values from -6 to 6
- values: bfloat16 [4096, 8192], P(('stretch', 'ctx')), may hold values from -6 to 6
- filters: float32 [256, 4096], P('ctx'), may hold values from -0.09375 to 0.09375
- skip_bias: float32 [8192], P('ctx'), may hold values from -1 to 1
- doc_blocks: int32 [16], replicated, may hold values from 1 to 12, 32 in all
Outputs:
- output: bfloat16 [4096, 8192], P(('stretch', 'ctx'))
Inputs may be any that keep to these rules, and one draw needn't show every extreme that they name: doc_blocks sum to 32; the largest is exactly 12.
All inputs are finite; a program needn't handle non-finite values.
Results may differ from a plain program's by a relative error of at most 0.0057.
Values may be sent and summed in bfloat16 or wider, within the bound.
A program may use at most 128 MiB of HBM per device.

v0:
```python
import functools
import math

import jax
import jax.numpy as jnp
from jax import lax
from jax.experimental import pallas as pl
from jax.experimental.pallas import tpu as pltpu
from jax.sharding import PartitionSpec as P

BLK = 128
TILE_BLOCKS = 8
MESH = pl.DeviceIdType.MESH


def kernel(
    stretch, ctx, chunks, lags, width,
    pre_ref, val_ref, post_ref, filt_ref, skip_ref, live_ref, out_ref,
    gated, arrived, mixed, back, toeplitz,
    send_in, recv_in, send_back, recv_back,
):
    n = stretch * ctx
    me = lax.axis_index("stretch") * ctx + lax.axis_index("ctx")
    rows = gated.shape[2]
    share = chunks * rows
    chunk_groups = rows // width
    stride = 5 if math.gcd(5, n) == 1 else 1

    def peer(k):
        return lax.rem(me + k * stride, n)

    def place(device):
        return (device // ctx, lax.rem(device, ctx))

    def slab_of(device):
        return lax.rem(device, ctx) * stretch + device // ctx

    barrier = pltpu.get_barrier_semaphore()

    @pl.loop(1, n)
    def _(k):
        pl.semaphore_signal(barrier, inc=1, device_id=place(peer(k)), device_id_type=MESH)

    unit = max(share, BLK)

    @pl.loop(0, n * share // unit)
    def _(tile):
        lanes = pl.ds(pl.multiple_of(tile * unit, unit), unit)
        product = pre_ref[:, lanes].astype(jnp.float32) * val_ref[:, lanes].astype(jnp.float32)
        turned = product.T.astype(jnp.bfloat16)
        for device in range(unit // share):
            for chunk in range(chunks):
                first = device * share + chunk * rows
                gated[chunk, tile * (unit // share) + device] = turned[first : first + rows]

    pl.semaphore_wait(barrier, n - 1)

    def copy_in(chunk, device, slot):
        return pltpu.make_async_remote_copy(
            src_ref=gated.at[chunk, slab_of(device)],
            dst_ref=arrived.at[chunk, slot],
            send_sem=send_in.at[chunk, device],
            recv_sem=recv_in.at[chunk, slot],
            device_id=place(device),
            device_id_type=MESH,
        )

    def copy_back(chunk, device, slot):
        return pltpu.make_async_remote_copy(
            src_ref=mixed.at[chunk, device],
            dst_ref=back.at[chunk, slot],
            send_sem=send_back.at[chunk, device],
            recv_sem=recv_back.at[chunk, slot],
            device_id=place(device),
            device_id_type=MESH,
        )

    for chunk in range(chunks):

        @pl.loop(1, n)
        def _(k, chunk=chunk):
            copy_in(chunk, peer(k), me).start()

    for chunk in range(chunks):
        arrived[chunk, me] = gated[chunk, slab_of(me)]

    @pl.loop(0, chunks * chunk_groups)
    def _(group):
        for lag in range(lags):
            taps = filt_ref[pl.ds(group, 1), lag * BLK : (lag + 2) * BLK]
            spread = jnp.broadcast_to(taps, (BLK, 2 * BLK))
            turned = pltpu.roll(spread, 0, 1, stride=1, stride_axis=0)
            toeplitz[group, lag * BLK : (lag + 1) * BLK, :] = turned[:, BLK:].astype(jnp.bfloat16)

    for chunk in range(chunks):

        @pl.loop(1, n)
        def _(k, chunk=chunk):
            copy_in(chunk, me, peer(k)).wait_recv()

        @pl.loop(0, chunk_groups * (n // TILE_BLOCKS))
        def _(step, chunk=chunk):
            group = step // (n // TILE_BLOCKS)
            first = lax.rem(step, n // TILE_BLOCKS) * TILE_BLOCKS
            channels = pl.ds(pl.multiple_of(group * width, width), width)
            columns = []
            for lag in range(lags):
                pieces = []
                for block in range(TILE_BLOCKS):
                    source = lax.rem(first + (block - lag + n), n)
                    live = live_ref[first + block, lag]
                    live = jnp.concatenate([live] * (width // live.shape[0]), axis=0)
                    pieces.append(arrived[chunk, source, channels, :] * live)
                columns.append(jnp.concatenate(pieces, axis=0))
            window = jnp.concatenate(columns, axis=1)
            conv = jnp.dot(
                window, toeplitz[chunk * chunk_groups + group], preferred_element_type=jnp.float32
            )
            skip = skip_ref[pl.ds(pl.multiple_of(chunk * rows + group * width, width), width), :]
            for block in range(TILE_BLOCKS):
                direct = arrived[chunk, first + block, channels, :].astype(jnp.float32)
                total = conv[block * width : (block + 1) * width] + skip * direct
                mixed[chunk, first + block, channels, :] = total.astype(jnp.bfloat16)

        @pl.loop(1, n)
        def _(k, chunk=chunk):
            copy_back(chunk, peer(k), me).start()

        back[chunk, me] = mixed[chunk, me]

    def finish(lanes, turned):
        product = turned.astype(jnp.float32).T * post_ref[:, lanes].astype(jnp.float32)
        out_ref[:, lanes] = product.astype(jnp.bfloat16)

    for chunk in range(chunks):

        @pl.loop(0, n)
        def _(k, chunk=chunk):
            device = peer(k)

            @pl.when(k > 0)
            def _():
                copy_back(chunk, me, device).wait_recv()

            if rows % BLK == 0:
                lanes = pl.ds(pl.multiple_of(slab_of(device) * share + chunk * rows, BLK), rows)
                finish(lanes, back[chunk, device])

    if rows % BLK != 0:
        per = BLK // rows

        @pl.loop(0, n // per)
        def _(tile):
            slabs = [tile * per + index for index in range(per)]
            pieces = [back[0, lax.rem(slab, stretch) * ctx + slab // stretch] for slab in slabs]
            turned = jnp.concatenate(pieces, axis=0)
            finish(pl.ds(pl.multiple_of(tile * BLK, BLK), BLK), turned)

    for chunk in range(chunks):

        @pl.loop(1, n)
        def _(k, chunk=chunk):
            copy_in(chunk, peer(k), me).wait_send()
            copy_back(chunk, peer(k), me).wait_send()


def per_device(stretch, ctx, post_gate, pre_gate, values, filters, skip_bias, doc_blocks):
    n = stretch * ctx
    tok_rows, model = values.shape
    taps = filters.shape[1]
    share = model // n
    groups = filters.shape[0] // stretch
    width = share // groups
    blocks = n * tok_rows // BLK
    longest = blocks * 3 // 8
    lags = min(longest, taps // BLK + 1)
    chunks = share // BLK if share % BLK == 0 else 1
    rows = share // chunks
    part = lax.axis_index("stretch")
    own_filters = lax.dynamic_slice_in_dim(filters, part * groups, groups, 0)
    own_filters = jnp.pad(own_filters, ((0, 0), (BLK, BLK)))
    own_skip = lax.dynamic_slice_in_dim(skip_bias, part * share, share, 0)
    own_skip = jnp.broadcast_to(own_skip[:, None], (share, BLK))
    ids = jnp.arange(blocks, dtype=jnp.int32)
    ends = jnp.cumsum(doc_blocks)
    starts = jnp.max(jnp.where(ends[None, :] <= ids[:, None], ends[None, :], 0), axis=1)
    live = (ids[:, None] - jnp.arange(lags, dtype=jnp.int32)[None, :]) >= starts[:, None]
    live = jnp.broadcast_to(live.astype(jnp.bfloat16)[:, :, None, None], (blocks, lags, 16, BLK))
    slab = (chunks, n, rows, BLK)
    vmem = pl.BlockSpec(memory_space=pltpu.VMEM)
    sems = pltpu.SemaphoreType.DMA((chunks, n))
    return pl.pallas_call(
        functools.partial(kernel, stretch, ctx, chunks, lags, width),
        out_shape=jax.ShapeDtypeStruct((tok_rows, model), jnp.bfloat16),
        in_specs=[vmem] * 6,
        out_specs=vmem,
        scratch_shapes=[
            pltpu.VMEM(slab, jnp.bfloat16),
            pltpu.VMEM(slab, jnp.bfloat16),
            pltpu.VMEM(slab, jnp.bfloat16),
            pltpu.VMEM(slab, jnp.bfloat16),
            pltpu.VMEM((groups, lags * BLK, BLK), jnp.bfloat16),
            sems, sems, sems, sems,
        ],
        compiler_params=pltpu.CompilerParams(
            collective_id=0, has_side_effects=True, vmem_limit_bytes=56 * 1024 * 1024
        ),
    )(pre_gate, values, post_gate, own_filters, own_skip, live)


def solution(mesh):
    rows = P(("stretch", "ctx"), None)
    body = functools.partial(per_device, mesh.shape["stretch"], mesh.shape["ctx"])
    return jax.shard_map(
        body,
        mesh=mesh,
        in_specs=(rows, rows, rows, P("ctx", None), P("ctx"), P()),
        out_specs=rows,
        check_vma=False,
    )
```

profile of v0, /device:TPU:0, one launch (start us, length us, event | category | flops | bytes accessed | tf_op | source)
XLA Modules:
  0.0 117.7 jit_solution(5923587933934318669)
XLA Ops:
  0.0 0.0 copy-start
  0.0 0.8 dynamic_slice.7
  0.8 0.7 copy.9
  1.6 0.1 reduce
  1.7 0.1 select_reduce_fusion
  1.8 0.1 fusion
  1.9 0.8 broadcast_in_dim.10.skip_ref
  2.6 0.0 copy-done
  2.6 0.7 pad.4.filt_ref
  3.3 1.6 %broadcast_in_dim.16.live_ref = bf16[32,12,16,128]{3,2,1,0:T(8,128)(2,1)} broadcast(bf16[32,12]{1,0:T(8,128)(2,1)S(1)} %fusion), dimensions={0,1} | broadcast | bytes 1573632 | tf_op jit(solution)/shard_map/broadcast_in_dim | solution.py:188
  4.9 109.6 %shard_map.64 = bf16[128,8192]{1,0:T(8,128)(2,1)} custom-call(bf16[128,8192]{1,0:T(8,128)(2,1)} %pre_ref.1, bf16[128,8192]{1,0:T(8,128)(2,1)} %val_ref.1, bf16[128,8192]{1,0:T(8,128)(2,1)} %post_ref.1, f32[8,4352]{1,0:T(8,128)} %pad.4.filt_ref, f32[256,128]{1,0:T(8,128)} %broadcast_in_dim.10.skip_ref, bf16[32,12,16,128]{3,2,1,0:T(8,128)(2,1)} %broadcast_in_dim.16.live_ref), custom_call_target="tpu_custom_call" | custom-call | tf_op jit(solution)/shard_map/pallas_call | solution.py:192
  114.6 3.1 %copy.11 = bf16[128,8192]{1,0:T(8,128)(2,1)} copy(bf16[128,8192]{1,0:T(8,128)(2,1)} %shard_map.64) | data formatting | bytes 4194304
  (2 shorter events, 0.0 us)
Async XLA Ops:
  0.0 2.6 %copy-start = (f32[32,4096]{1,0:T(8,128)S(1)}, f32[32,4096]{1,0:T(8,128)}, u32[]{:S(2)}) copy-start(f32[32,4096]{1,0:T(8,128)} %param.9) | copy-start | bytes 1572868
where the time goes:
time: 118 us
  Pallas kernels  110 us (93%)
  local copies, waits for them, and re-layouts  7.71 us (7%)
    pallas_call x1, Pallas kernels, per_device(): pl.pallas_call(functools.partial(kernel, stretch, ctx, chunks, lags, widt...  110 us
    unnamed x3, local copies, waits for them, and re-layouts  3.1 us

commit v1 on v0

--- a/solution.py
+++ b/solution.py
@@ -15,10 +15,17 @@
 
 def kernel(
     stretch, ctx, chunks, lags, width,
-    pre_ref, val_ref, post_ref, filt_ref, skip_ref, live_ref, out_ref,
-    gated, arrived, mixed, back, toeplitz,
-    send_in, recv_in, send_back, recv_back,
+    pre_ref, val_ref, filt_ref, skip_ref, docs_ref, out_ref,
+    pre, val, gated, arrived, mixed, back, toeplitz, skips, live,
+    load_sem, send_in, recv_in, send_back, recv_back,
 ):
+    loads = [
+        pltpu.make_async_copy(pre_ref, pre, load_sem.at[0]),
+        pltpu.make_async_copy(val_ref, val, load_sem.at[1]),
+    ]
+    for load in loads:
+        load.start()
+    part = lax.axis_index("stretch")
     n = stretch * ctx
     me = lax.axis_index("stretch") * ctx + lax.axis_index("ctx")
     rows = gated.shape[2]
@@ -40,20 +47,6 @@
     @pl.loop(1, n)
     def _(k):
         pl.semaphore_signal(barrier, inc=1, device_id=place(peer(k)), device_id_type=MESH)
-
-    unit = max(share, BLK)
-
-    @pl.loop(0, n * share // unit)
-    def _(tile):
-        lanes = pl.ds(pl.multiple_of(tile * unit, unit), unit)
-        product = pre_ref[:, lanes].astype(jnp.float32) * val_ref[:, lanes].astype(jnp.float32)
-        turned = product.T.astype(jnp.bfloat16)
-        for device in range(unit // share):
-            for chunk in range(chunks):
-                first = device * share + chunk * rows
-                gated[chunk, tile * (unit // share) + device] = turned[first : first + rows]
-
-    pl.semaphore_wait(barrier, n - 1)
 
     def copy_in(chunk, device, slot):
         return pltpu.make_async_remote_copy(
@@ -75,22 +68,86 @@
             device_id_type=MESH,
         )
 
-    for chunk in range(chunks):
-
-        @pl.loop(1, n)
-        def _(k, chunk=chunk):
-            copy_in(chunk, peer(k), me).start()
+    unit = max(share, BLK)
+    per_unit = unit // share
+
+    def gate(tile):
+        lanes = pl.ds(pl.multiple_of(tile * unit, unit), unit)
+        product = pre[:, lanes].astype(jnp.float32) * val[:, lanes].astype(jnp.float32)
+        turned = product.T.astype(jnp.bfloat16)
+        for slab in range(per_unit):
+            for chunk in range(chunks):
+                first = slab * share + chunk * rows
+                gated[chunk, tile * per_unit + slab] = turned[first : first + rows]
+
+    for load in loads:
+        load.wait()
+    early = n // 4 if per_unit == 1 else n
+
+    if per_unit == 1:
+
+        @pl.loop(0, early)
+        def _(k):
+            gate(slab_of(peer(k)))
+
+    else:
+
+        @pl.loop(0, n // per_unit)
+        def _(tile):
+            gate(tile)
+
+    pl.semaphore_wait(barrier, n - 1)
+
+    @pl.loop(1, early)
+    def _(k):
+        copy_in(0, peer(k), me).start()
+
+    @pl.loop(early, n)
+    def _(k):
+        gate(slab_of(peer(k)))
+        copy_in(0, peer(k), me).start()
 
     for chunk in range(chunks):
         arrived[chunk, me] = gated[chunk, slab_of(me)]
+
+    taps = filt_ref.shape[1]
 
     @pl.loop(0, chunks * chunk_groups)
     def _(group):
+        row = part * (chunks * chunk_groups) + group
+        chosen = lax.broadcasted_iota(jnp.int32, (filt_ref.shape[0], BLK), 0) == row
         for lag in range(lags):
-            taps = filt_ref[pl.ds(group, 1), lag * BLK : (lag + 2) * BLK]
-            spread = jnp.broadcast_to(taps, (BLK, 2 * BLK))
+            pieces = []
+            for first in ((lag - 1) * BLK, lag * BLK):
+                if 0 <= first < taps:
+                    picked = jnp.where(chosen, filt_ref[:, first : first + BLK], 0.0)
+                    pieces.append(jnp.sum(picked, axis=0, keepdims=True))
+                else:
+                    pieces.append(jnp.zeros((1, BLK), jnp.float32))
+            spread = jnp.broadcast_to(jnp.concatenate(pieces, axis=1), (BLK, 2 * BLK))
             turned = pltpu.roll(spread, 0, 1, stride=1, stride_axis=0)
             toeplitz[group, lag * BLK : (lag + 1) * BLK, :] = turned[:, BLK:].astype(jnp.bfloat16)
+
+    skips[...] = jnp.broadcast_to(skip_ref[pl.ds(part, 1), :], (BLK, share)).T
+    ends = []
+    for doc in range(docs_ref.shape[0]):
+        ends.append(docs_ref[doc] + (ends[-1] if ends else 0))
+
+    @pl.loop(0, n)
+    def _(block):
+        start = jnp.int32(0)
+        for end in ends:
+            start = jnp.maximum(start, jnp.where(end <= block, end, 0))
+        for lag in range(lags):
+            weight = jnp.where(block - lag >= start, 1.0, 0.0).astype(jnp.float32)
+            live[block, lag] = jnp.full(live.shape[2:], weight, jnp.float32).astype(jnp.bfloat16)
+
+    for chunk in range(1, chunks):
+
+        @pl.loop(1, n)
+        def _(k, chunk=chunk):
+            copy_in(chunk - 1, peer(k), me).wait_send()
+            copy_in(chunk, peer(k), me).start()
 
     for chunk in range(chunks):
 
@@ -108,15 +165,14 @@
                 pieces = []
                 for block in range(TILE_BLOCKS):
                     source = lax.rem(first + (block - lag + n), n)
-                    live = live_ref[first + block, lag]
-                    live = jnp.concatenate([live] * (width // live.shape[0]), axis=0)
-                    pieces.append(arrived[chunk, source, channels, :] * live)
+                    kept = jnp.concatenate([live[first + block, lag]] * (width // live.shape[2]), axis=0)
+                    pieces.append(arrived[chunk, source, channels, :] * kept)
                 columns.append(jnp.concatenate(pieces, axis=0))
             window = jnp.concatenate(columns, axis=1)
             conv = jnp.dot(
                 window, toeplitz[chunk * chunk_groups + group], preferred_element_type=jnp.float32
             )
-            skip = skip_ref[pl.ds(pl.multiple_of(chunk * rows + group * width, width), width), :]
+            skip = skips[pl.ds(pl.multiple_of(chunk * rows + group * width, width), width), :]
             for block in range(TILE_BLOCKS):
                 direct = arrived[chunk, first + block, channels, :].astype(jnp.float32)
                 total = conv[block * width : (block + 1) * width] + skip * direct
@@ -124,13 +180,14 @@
 
         @pl.loop(1, n)
         def _(k, chunk=chunk):
+            if chunk == 0:
+                copy_in(chunks - 1, peer(k), me).wait_send()
             copy_back(chunk, peer(k), me).start()
 
         back[chunk, me] = mixed[chunk, me]
 
     def finish(lanes, turned):
-        product = turned.astype(jnp.float32).T * post_ref[:, lanes].astype(jnp.float32)
-        out_ref[:, lanes] = product.astype(jnp.bfloat16)
+        out_ref[:, lanes] = turned.astype(jnp.float32).T.astype(jnp.bfloat16)
 
     for chunk in range(chunks):
 
@@ -160,7 +217,6 @@
 
         @pl.loop(1, n)
         def _(k, chunk=chunk):
-            copy_in(chunk, peer(k), me).wait_send()
             copy_back(chunk, peer(k), me).wait_send()
 
 
@@ -176,36 +232,38 @@
     lags = min(longest, taps // BLK + 1)
     chunks = share // BLK if share % BLK == 0 else 1
     rows = share // chunks
-    part = lax.axis_index("stretch")
-    own_filters = lax.dynamic_slice_in_dim(filters, part * groups, groups, 0)
-    own_filters = jnp.pad(own_filters, ((0, 0), (BLK, BLK)))
-    own_skip = lax.dynamic_slice_in_dim(skip_bias, part * share, share, 0)
-    own_skip = jnp.broadcast_to(own_skip[:, None], (share, BLK))
-    ids = jnp.arange(blocks, dtype=jnp.int32)
-    ends = jnp.cumsum(doc_blocks)
-    starts = jnp.max(jnp.where(ends[None, :] <= ids[:, None], ends[None, :], 0), axis=1)
-    live = (ids[:, None] - jnp.arange(lags, dtype=jnp.int32)[None, :]) >= starts[:, None]
-    live = jnp.broadcast_to(live.astype(jnp.bfloat16)[:, :, None, None], (blocks, lags, 16, BLK))
     slab = (chunks, n, rows, BLK)
     vmem = pl.BlockSpec(memory_space=pltpu.VMEM)
     sems = pltpu.SemaphoreType.DMA((chunks, n))
-    return pl.pallas_call(
+    returned = pl.pallas_call(
         functools.partial(kernel, stretch, ctx, chunks, lags, width),
         out_shape=jax.ShapeDtypeStruct((tok_rows, model), jnp.bfloat16),
-        in_specs=[vmem] * 6,
+        in_specs=[
+            pl.BlockSpec(memory_space=pltpu.HBM),
+            pl.BlockSpec(memory_space=pltpu.HBM),
+            vmem,
+            vmem,
+            pl.BlockSpec(memory_space=pltpu.SMEM),
+        ],
         out_specs=vmem,
         scratch_shapes=[
+            pltpu.VMEM((tok_rows, model), jnp.bfloat16),
+            pltpu.VMEM((tok_rows, model), jnp.bfloat16),
             pltpu.VMEM(slab, jnp.bfloat16),
             pltpu.VMEM(slab, jnp.bfloat16),
             pltpu.VMEM(slab, jnp.bfloat16),
             pltpu.VMEM(slab, jnp.bfloat16),
             pltpu.VMEM((groups, lags * BLK, BLK), jnp.bfloat16),
+            pltpu.VMEM((share, BLK), jnp.float32),
+            pltpu.VMEM((blocks, lags, 16, BLK), jnp.bfloat16),
+            pltpu.SemaphoreType.DMA((2,)),
             sems, sems, sems, sems,
         ],
         compiler_params=pltpu.CompilerParams(
-            collective_id=0, has_side_effects=True, vmem_limit_bytes=56 * 1024 * 1024
+            collective_id=0, has_side_effects=True, vmem_limit_bytes=44 * 1024 * 1024
         ),
-    )(pre_gate, values, post_gate, own_filters, own_skip, live)
+    )(pre_gate, values, filters, skip_bias.reshape(stretch, share), doc_blocks)
+    return (post_gate.astype(jnp.float32) * returned.astype(jnp.float32)).astype(jnp.bfloat16)
 
 
 def solution(mesh):

time: 118 us -> 113 us (0.958)
  Pallas kernels: 110 us -> 106 us
  local copies, waits for them, and re-layouts: 7.71 us -> 5.57 us
  other arithmetic: 0.32 us -> 1.81 us
    pallas_call x1, Pallas kernels: 110 us -> 106 us  [per_device(): pl.pallas_call(functools.partial(kernel, stretch, ctx, chunks, lags, widt...]
    broadcast_in_dim x2 -> x0, local copies, waits for them, and re-layouts: 2.37 us -> none  [the longest x1 1.61 us: per_device(): jnp.broadcast_to(live.astype(jnp.bfloat16)[:, :, None, None], (blocks, la...]
    unnamed x3 -> x10, local copies, waits for them, and re-layouts: 3.1 us -> 4.88 us
    convert_element_type x1, other arithmetic: 0.08 us -> 1.81 us  [per_device(): (post_gate.astype(jnp.float32) * returned.astype(jnp.float32)).astype(jnp...]
where the time goes in v1:
time: 113 us
  Pallas kernels  106 us (94%)
  local copies, waits for them, and re-layouts  5.57 us (5%)
  other arithmetic  1.81 us (2%)
    pallas_call x1, Pallas kernels, per_device(): pl.pallas_call(functools.partial(kernel, stretch, ctx, chunks, lags, widt...  106 us
    unnamed x10, local copies, waits for them, and re-layouts  4.88 us

profile of v1, /device:TPU:0, one launch (start us, length us, event | category | flops | bytes accessed | tf_op | source)
XLA Modules:
  0.0 113.1 jit_solution(17331409853458728120)
XLA Ops:
  0.0 0.7 reshape.3.skip_ref
  0.7 0.0 copy-start
  0.7 1.6 %copy-done = bf16[128,8192]{1,0:T(8,128)(2,1)S(1)} copy-done((bf16[128,8192]{1,0:T(8,128)(2,1)S(1)}, bf16[128,8192]{1,0:T(8,128)(2,1)}, u32[]{:S(2)}) %copy-start) | copy-done | bytes 2097176
  2.3 0.0 copy-start.1
  2.3 1.6 %copy-done.1 = bf16[128,8192]{1,0:T(8,128)(2,1)S(1)} copy-done((bf16[128,8192]{1,0:T(8,128)(2,1)S(1)}, bf16[128,8192]{1,0:T(8,128)(2,1)}, u32[]{:S(2)}) %copy-start.1) | copy-done | bytes 2097176
  3.9 0.0 copy-start.2
  3.9 1.0 copy-done.2
  4.9 0.0 copy-start.3
  4.9 0.7 copy-done.3
  5.6 0.0 copy-start.4
  5.6 105.7 %shard_map.64 = bf16[128,8192]{1,0:T(8,128)(2,1)S(1)} custom-call(bf16[128,8192]{1,0:T(8,128)(2,1)S(1)} %copy-done, bf16[128,8192]{1,0:T(8,128)(2,1)S(1)} %copy-done.1, f32[32,4096]{1,0:T(8,128)S(1)} %copy-done.2, f32[4,256]{1,0:T(4,128)S(1)} %reshape.3.skip_ref, s32[16]{0:T(128)S(1)} %copy-done.3), custom_call_target="tpu_custom_call" | custom-call | tf_op jit(solution)/shard_map/pallas_call | solution.py:238
  111.3 0.0 copy-done.4
  111.3 1.8 %multiply_convert_fusion = bf16[128,8192]{1,0:T(8,128)(2,1)} fusion(bf16[128,8192]{1,0:T(8,128)(2,1)S(1)} %shard_map.64, bf16[128,8192]{1,0:T(8,128)(2,1)S(1)} %copy-done.4), kind=kLoop, calls=%fused_computation | loop fusion | flops 4194304 | bytes 6291456 | tf_op jit(solution)/shard_map/convert_element_type | solution.py:266
Async XLA Ops:
  0.7 1.6 %copy-start = (bf16[128,8192]{1,0:T(8,128)(2,1)S(1)}, bf16[128,8192]{1,0:T(8,128)(2,1)}, u32[]{:S(2)}) copy-start(bf16[128,8192]{1,0:T(8,128)(2,1)} %pre_ref.1) | copy-start | bytes 6291460
  2.3 1.6 %copy-start.1 = (bf16[128,8192]{1,0:T(8,128)(2,1)S(1)}, bf16[128,8192]{1,0:T(8,128)(2,1)}, u32[]{:S(2)}) copy-start(bf16[128,8192]{1,0:T(8,128)(2,1)} %val_ref.1) | copy-start | bytes 6291460
  3.9 1.0 copy-start.2
  4.9 0.7 copy-start.3
  5.6 105.7 %copy-start.4 = (bf16[128,8192]{1,0:T(8,128)(2,1)S(1)}, bf16[128,8192]{1,0:T(8,128)(2,1)}, u32[]{:S(2)}) copy-start(bf16[128,8192]{1,0:T(8,128)(2,1)} %param.6) | copy-start | bytes 6291460

commit v2 on v1

--- a/solution.py
+++ b/solution.py
@@ -1,5 +1,4 @@
 import functools
-import math
 
 import jax
 import jax.numpy as jnp
@@ -16,12 +15,13 @@
 def kernel(
     stretch, ctx, chunks, lags, width,
     pre_ref, val_ref, filt_ref, skip_ref, docs_ref, out_ref,
-    pre, val, gated, arrived, mixed, back, toeplitz, skips, live,
+    pre, val, filt, gated, arrived, mixed, back, toeplitz, skips, live,
     load_sem, send_in, recv_in, send_back, recv_back,
 ):
     loads = [
         pltpu.make_async_copy(pre_ref, pre, load_sem.at[0]),
         pltpu.make_async_copy(val_ref, val, load_sem.at[1]),
+        pltpu.make_async_copy(filt_ref, filt, load_sem.at[2]),
     ]
     for load in loads:
         load.start()
@@ -31,10 +31,15 @@
     rows = gated.shape[2]
     share = chunks * rows
     chunk_groups = rows // width
-    stride = 5 if math.gcd(5, n) == 1 else 1
+    halves = 2 if ctx % 2 == 0 else 1
+    half = ctx // halves
+    my_part, my_place = lax.axis_index("stretch"), lax.axis_index("ctx")
 
     def peer(k):
-        return lax.rem(me + k * stride, n)
+        step = k // halves
+        column = lax.rem(my_part + lax.rem(step, stretch), stretch)
+        side = lax.rem(my_place // half + lax.rem(k, halves), halves)
+        return column * ctx + side * half + lax.rem(lax.rem(my_place, half) + step // stretch, half)
 
     def place(device):
         return (device // ctx, lax.rem(device, ctx))
@@ -80,7 +85,7 @@
                 first = slab * share + chunk * rows
                 gated[chunk, tile * per_unit + slab] = turned[first : first + rows]
 
-    for load in loads:
+    for load in loads[:2]:
         load.wait()
     early = n // 4 if per_unit == 1 else n
 
@@ -110,17 +115,18 @@
     for chunk in range(chunks):
         arrived[chunk, me] = gated[chunk, slab_of(me)]
 
-    taps = filt_ref.shape[1]
+    loads[2].wait()
+    taps = filt.shape[1]
 
     @pl.loop(0, chunks * chunk_groups)
     def _(group):
         row = part * (chunks * chunk_groups) + group
-        chosen = lax.broadcasted_iota(jnp.int32, (filt_ref.shape[0], BLK), 0) == row
+        chosen = lax.broadcasted_iota(jnp.int32, (filt.shape[0], BLK), 0) == row
         for lag in range(lags):
             pieces = []
             for first in ((lag - 1) * BLK, lag * BLK):
                 if 0 <= first < taps:
-                    picked = jnp.where(chosen, filt_ref[:, first : first + BLK], 0.0)
+                    picked = jnp.where(chosen, filt[:, first : first + BLK], 0.0)
                     pieces.append(jnp.sum(picked, axis=0, keepdims=True))
                 else:
                     pieces.append(jnp.zeros((1, BLK), jnp.float32))
@@ -128,7 +134,7 @@
             turned = pltpu.roll(spread, 0, 1, stride=1, stride_axis=0)
             toeplitz[group, lag * BLK : (lag + 1) * BLK, :] = turned[:, BLK:].astype(jnp.bfloat16)
 
-    skips[...] = jnp.broadcast_to(skip_ref[pl.ds(part, 1), :], (BLK, share)).T
+    skips[...] = jnp.broadcast_to(skip_ref[...].reshape(1, stretch * share), (BLK, stretch * share)).T
     ends = []
     for doc in range(docs_ref.shape[0]):
         ends.append(docs_ref[doc] + (ends[-1] if ends else 0))
@@ -142,14 +148,19 @@
             weight = jnp.where(block - lag >= start, 1.0, 0.0).astype(jnp.float32)
             live[block, lag] = jnp.full(live.shape[2:], weight, jnp.float32).astype(jnp.bfloat16)
 
-    for chunk in range(1, chunks):
+    if chunks > 1:
+
+        @pl.loop(1, n)
+        def _(k):
+            copy_in(1, peer(k), me).start()
+
+    for chunk in range(chunks):
 
         @pl.loop(1, n)
         def _(k, chunk=chunk):
-            copy_in(chunk - 1, peer(k), me).wait_send()
-            copy_in(chunk, peer(k), me).start()
-
-    for chunk in range(chunks):
+            if chunk + 2 < chunks:
+                copy_in(chunk, peer(k), me).wait_send()
+                copy_in(chunk + 2, peer(k), me).start()
 
         @pl.loop(1, n)
         def _(k, chunk=chunk):
@@ -172,51 +183,63 @@
             conv = jnp.dot(
                 window, toeplitz[chunk * chunk_groups + group], preferred_element_type=jnp.float32
             )
-            skip = skips[pl.ds(pl.multiple_of(chunk * rows + group * width, width), width), :]
+            skip_row = part * share + chunk * rows + group * width
+            skip = skips[pl.ds(pl.multiple_of(skip_row, width), width), :]
             for block in range(TILE_BLOCKS):
                 direct = arrived[chunk, first + block, channels, :].astype(jnp.float32)
                 total = conv[block * width : (block + 1) * width] + skip * direct
                 mixed[chunk, first + block, channels, :] = total.astype(jnp.bfloat16)
 
-        @pl.loop(1, n)
-        def _(k, chunk=chunk):
-            if chunk == 0:
-                copy_in(chunks - 1, peer(k), me).wait_send()
-            copy_back(chunk, peer(k), me).start()
-
         back[chunk, me] = mixed[chunk, me]
+
+        if chunk == chunks - 2:
+            ready = range(chunks - 1)
+        else:
+            ready = [chunk] if chunk == chunks - 1 else []
+        for done in ready:
+
+            @pl.loop(1, n)
+            def _(k, done=done):
+                copy_back(done, peer(k), me).start()
 
     def finish(lanes, turned):
         out_ref[:, lanes] = turned.astype(jnp.float32).T.astype(jnp.bfloat16)
 
+    joint = max(BLK // rows, 1)
+    if share % BLK == 0:
+        for first in range(0, chunks, joint):
+
+            @pl.loop(0, n)
+            def _(k, first=first):
+                device = peer(k)
+
+                @pl.when(k > 0)
+                def _():
+                    for chunk in range(first, first + joint):
+                        copy_back(chunk, me, device).wait_recv()
+
+                pieces = [back[chunk, device] for chunk in range(first, first + joint)]
+                lane = slab_of(device) * share + first * rows
+                finish(pl.ds(pl.multiple_of(lane, BLK), joint * rows), jnp.concatenate(pieces, axis=0))
+
+    else:
+
+        @pl.loop(1, n)
+        def _(k):
+            copy_back(0, me, peer(k)).wait_recv()
+
+        @pl.loop(0, n // joint)
+        def _(tile):
+            slabs = [tile * joint + index for index in range(joint)]
+            pieces = [back[0, lax.rem(slab, stretch) * ctx + slab // stretch] for slab in slabs]
+            finish(pl.ds(pl.multiple_of(tile * BLK, BLK), BLK), jnp.concatenate(pieces, axis=0))
+
     for chunk in range(chunks):
 
-        @pl.loop(0, n)
+        @pl.loop(1, n)
         def _(k, chunk=chunk):
-            device = peer(k)
-
-            @pl.when(k > 0)
-            def _():
-                copy_back(chunk, me, device).wait_recv()
-
-            if rows % BLK == 0:
-                lanes = pl.ds(pl.multiple_of(slab_of(device) * share + chunk * rows, BLK), rows)
-                finish(lanes, back[chunk, device])
-
-    if rows % BLK != 0:
-        per = BLK // rows
-
-        @pl.loop(0, n // per)
-        def _(tile):
-            slabs = [tile * per + index for index in range(per)]
-            pieces = [back[0, lax.rem(slab, stretch) * ctx + slab // stretch] for slab in slabs]
-            turned = jnp.concatenate(pieces, axis=0)
-            finish(pl.ds(pl.multiple_of(tile * BLK, BLK), BLK), turned)
-
-    for chunk in range(chunks):
-
-        @pl.loop(1, n)
-        def _(k, chunk=chunk):
+            if chunk + 2 >= chunks:
+                copy_in(chunk, peer(k), me).wait_send()
             copy_back(chunk, peer(k), me).wait_send()
 
 
@@ -230,7 +253,7 @@
     blocks = n * tok_rows // BLK
     longest = blocks * 3 // 8
     lags = min(longest, taps // BLK + 1)
-    chunks = share // BLK if share % BLK == 0 else 1
+    chunks = share // (2 * width) if share % BLK == 0 else 1
     rows = share // chunks
     slab = (chunks, n, rows, BLK)
     vmem = pl.BlockSpec(memory_space=pltpu.VMEM)
@@ -241,7 +264,7 @@
         in_specs=[
             pl.BlockSpec(memory_space=pltpu.HBM),
             pl.BlockSpec(memory_space=pltpu.HBM),
-            vmem,
+            pl.BlockSpec(memory_space=pltpu.HBM),
             vmem,
             pl.BlockSpec(memory_space=pltpu.SMEM),
         ],
@@ -249,20 +272,21 @@
         scratch_shapes=[
             pltpu.VMEM((tok_rows, model), jnp.bfloat16),
             pltpu.VMEM((tok_rows, model), jnp.bfloat16),
+            pltpu.VMEM(filters.shape, jnp.float32),
             pltpu.VMEM(slab, jnp.bfloat16),
             pltpu.VMEM(slab, jnp.bfloat16),
             pltpu.VMEM(slab, jnp.bfloat16),
             pltpu.VMEM(slab, jnp.bfloat16),
             pltpu.VMEM((groups, lags * BLK, BLK), jnp.bfloat16),
-            pltpu.VMEM((share, BLK), jnp.float32),
+            pltpu.VMEM((stretch * share, BLK), jnp.float32),
             pltpu.VMEM((blocks, lags, 16, BLK), jnp.bfloat16),
-            pltpu.SemaphoreType.DMA((2,)),
+            pltpu.SemaphoreType.DMA((3,)),
             sems, sems, sems, sems,
         ],
         compiler_params=pltpu.CompilerParams(
-            collective_id=0, has_side_effects=True, vmem_limit_bytes=44 * 1024 * 1024
+            collective_id=0, has_side_effects=True, vmem_limit_bytes=62 * 1024 * 1024
         ),
-    )(pre_gate, values, filters, skip_bias.reshape(stretch, share), doc_blocks)
+    )(pre_gate, values, filters, skip_bias, doc_blocks)
     return (post_gate.astype(jnp.float32) * returned.astype(jnp.float32)).astype(jnp.bfloat16)
 
 

time: 113 us -> 116 us (1.027)
  Pallas kernels: 106 us -> 112 us
  local copies, waits for them, and re-layouts: 5.57 us -> 0 us
  other arithmetic: 1.81 us -> 4.04 us
    pallas_call x1, Pallas kernels: 106 us -> 112 us  [per_device(): pl.pallas_call(functools.partial(kernel, stretch, ctx, chunks, lags, widt...]
    unnamed x10 -> x0, local copies, waits for them, and re-layouts: 4.88 us -> none
    convert_element_type x1, other arithmetic: 1.81 us -> 4.04 us  [per_device(): (post_gate.astype(jnp.float32) * returned.astype(jnp.float32)).astype(jnp...]
where the time goes in v2:
time: 116 us
  Pallas kernels  112 us (97%)
  other arithmetic  4.04 us (3%)
    pallas_call x1, Pallas kernels, per_device(): pl.pallas_call(functools.partial(kernel, stretch, ctx, chunks, lags, widt...  112 us
    convert_element_type x1, other arithmetic, per_device(): (post_gate.astype(jnp.float32) * returned.astype(jnp.float32)).astype(jnp...  4.04 us

profile of v2, /device:TPU:0, one launch (start us, length us, event | category | flops | bytes accessed | tf_op | source)
XLA Modules:
  0.0 115.6 jit_solution(8995654045674123115)
XLA Ops:
  0.0 111.5 %shard_map.64 = bf16[128,8192]{1,0:T(8,128)(2,1)} custom-call(bf16[128,8192]{1,0:T(8,128)(2,1)} %pre_ref.1, bf16[128,8192]{1,0:T(8,128)(2,1)} %val_ref.1, f32[32,4096]{1,0:T(8,128)} %filt_ref.1, f32[1024]{0:T(1024)} %skip_ref.1, s32[16]{0:T(128)} %docs_ref.1), custom_call_target="tpu_custom_call" | custom-call | tf_op jit(solution)/shard_map/pallas_call | solution.py:261
  111.5 4.0 %multiply_convert_fusion = bf16[128,8192]{1,0:T(8,128)(2,1)} fusion(bf16[128,8192]{1,0:T(8,128)(2,1)} %shard_map.64, bf16[128,8192]{1,0:T(8,128)(2,1)} %param.6), kind=kLoop, calls=%fused_computation | loop fusion | flops 4194304 | bytes 6291456 | tf_op jit(solution)/shard_map/convert_element_type | solution.py:290

commit v3 on v2

--- a/solution.py
+++ b/solution.py
@@ -30,6 +30,7 @@
     me = lax.axis_index("stretch") * ctx + lax.axis_index("ctx")
     rows = gated.shape[2]
     share = chunks * rows
+    lead = lags - 1
     chunk_groups = rows // width
     halves = 2 if ctx % 2 == 0 else 1
     half = ctx // halves
@@ -56,7 +57,7 @@
     def copy_in(chunk, device, slot):
         return pltpu.make_async_remote_copy(
             src_ref=gated.at[chunk, slab_of(device)],
-            dst_ref=arrived.at[chunk, slot],
+            dst_ref=arrived.at[chunk, lead + slot],
             send_sem=send_in.at[chunk, device],
             recv_sem=recv_in.at[chunk, slot],
             device_id=place(device),
@@ -113,7 +114,8 @@
         copy_in(0, peer(k), me).start()
 
     for chunk in range(chunks):
-        arrived[chunk, me] = gated[chunk, slab_of(me)]
+        arrived[chunk, lead + me] = gated[chunk, slab_of(me)]
+        arrived[chunk, 0:lead] = jnp.zeros((lead, rows, BLK), jnp.bfloat16)
 
     loads[2].wait()
     taps = filt.shape[1]
@@ -158,9 +160,9 @@
 
         @pl.loop(1, n)
         def _(k, chunk=chunk):
-            if chunk + 2 < chunks:
-                copy_in(chunk, peer(k), me).wait_send()
-                copy_in(chunk + 2, peer(k), me).start()
+            if chunk == 0 and chunks > 2:
+                copy_in(0, peer(k), me).wait_send()
+                copy_in(2, peer(k), me).start()
 
         @pl.loop(1, n)
         def _(k, chunk=chunk):
@@ -175,7 +177,7 @@
             for lag in range(lags):
                 pieces = []
                 for block in range(TILE_BLOCKS):
-                    source = lax.rem(first + (block - lag + n), n)
+                    source = first + (lead + block - lag)
                     kept = jnp.concatenate([live[first + block, lag]] * (width // live.shape[2]), axis=0)
                     pieces.append(arrived[chunk, source, channels, :] * kept)
                 columns.append(jnp.concatenate(pieces, axis=0))
@@ -186,21 +188,22 @@
             skip_row = part * share + chunk * rows + group * width
             skip = skips[pl.ds(pl.multiple_of(skip_row, width), width), :]
             for block in range(TILE_BLOCKS):
-                direct = arrived[chunk, first + block, channels, :].astype(jnp.float32)
+                direct = arrived[chunk, first + (lead + block), channels, :].astype(jnp.float32)
                 total = conv[block * width : (block + 1) * width] + skip * direct
                 mixed[chunk, first + block, channels, :] = total.astype(jnp.bfloat16)
 
         back[chunk, me] = mixed[chunk, me]
 
-        if chunk == chunks - 2:
-            ready = range(chunks - 1)
-        else:
-            ready = [chunk] if chunk == chunks - 1 else []
-        for done in ready:
+        for later in range(3, chunks) if chunk == 0 else ():
 
             @pl.loop(1, n)
-            def _(k, done=done):
-                copy_back(done, peer(k), me).start()
+            def _(k, later=later):
+                copy_in(later - 2, peer(k), me).wait_send()
+                copy_in(later, peer(k), me).start()
+
+        @pl.loop(1, n)
+        def _(k, chunk=chunk):
+            copy_back(chunk, peer(k), me).start()
 
     def finish(lanes, turned):
         out_ref[:, lanes] = turned.astype(jnp.float32).T.astype(jnp.bfloat16)
@@ -274,7 +277,7 @@
             pltpu.VMEM((tok_rows, model), jnp.bfloat16),
             pltpu.VMEM(filters.shape, jnp.float32),
             pltpu.VMEM(slab, jnp.bfloat16),
-            pltpu.VMEM(slab, jnp.bfloat16),
+            pltpu.VMEM((chunks, lags - 1 + n, rows, BLK), jnp.bfloat16),
             pltpu.VMEM(slab, jnp.bfloat16),
             pltpu.VMEM(slab, jnp.bfloat16),
             pltpu.VMEM((groups, lags * BLK, BLK), jnp.bfloat16),
@@ -284,7 +287,7 @@
             sems, sems, sems, sems,
         ],
         compiler_params=pltpu.CompilerParams(
-            collective_id=0, has_side_effects=True, vmem_limit_bytes=62 * 1024 * 1024
+            collective_id=0, has_side_effects=True, vmem_limit_bytes=58 * 1024 * 1024
         ),
     )(pre_gate, values, filters, skip_bias, doc_blocks)
     return (post_gate.astype(jnp.float32) * returned.astype(jnp.float32)).astype(jnp.bfloat16)

time: 116 us -> 115 us (level)
  no operation moved by 1% of the time
where the time goes in v3:
time: 115 us
  Pallas kernels  111 us (97%)
  other arithmetic  3.41 us (3%)
    pallas_call x1, Pallas kernels, per_device(): pl.pallas_call(functools.partial(kernel, stretch, ctx, chunks, lags, widt...  111 us
    convert_element_type x1, other arithmetic, per_device(): (post_gate.astype(jnp.float32) * returned.astype(jnp.float32)).astype(jnp...  3.41 us

profile of v3, /device:TPU:0, one launch (start us, length us, event | category | flops | bytes accessed | tf_op | source)
XLA Modules:
  0.0 114.9 jit_solution(10681553909976714475)
XLA Ops:
  0.0 0.0 copy-start
  0.0 111.5 %shard_map.64 = bf16[128,8192]{1,0:T(8,128)(2,1)} custom-call(bf16[128,8192]{1,0:T(8,128)(2,1)} %pre_ref.1, bf16[128,8192]{1,0:T(8,128)(2,1)} %val_ref.1, f32[32,4096]{1,0:T(8,128)} %filt_ref.1, f32[1024]{0:T(1024)} %skip_ref.1, s32[16]{0:T(128)} %docs_ref.1), custom_call_target="tpu_custom_call" | custom-call | tf_op jit(solution)/shard_map/pallas_call | solution.py:264
  111.5 0.0 copy-done
  111.5 3.4 %multiply_convert_fusion = bf16[128,8192]{1,0:T(8,128)(2,1)} fusion(bf16[128,8192]{1,0:T(8,128)(2,1)} %shard_map.64, bf16[128,8192]{1,0:T(8,128)(2,1)S(1)} %copy-done), kind=kLoop, calls=%fused_computation | loop fusion | flops 4194304 | bytes 6291456 | tf_op jit(solution)/shard_map/convert_element_type | solution.py:293
Async XLA Ops:
  0.0 111.5 %copy-start = (bf16[128,8192]{1,0:T(8,128)(2,1)S(1)}, bf16[128,8192]{1,0:T(8,128)(2,1)}, u32[]{:S(2)}) copy-start(bf16[128,8192]{1,0:T(8,128)(2,1)} %param.6) | copy-start | bytes 6291460

commit v4 on v3

--- a/solution.py
+++ b/solution.py
@@ -1,4 +1,5 @@
 import functools
+import math
 
 import jax
 import jax.numpy as jnp
@@ -32,15 +33,10 @@
     share = chunks * rows
     lead = lags - 1
     chunk_groups = rows // width
-    halves = 2 if ctx % 2 == 0 else 1
-    half = ctx // halves
-    my_part, my_place = lax.axis_index("stretch"), lax.axis_index("ctx")
+    stride = 5 if math.gcd(5, n) == 1 else 1
 
     def peer(k):
-        step = k // halves
-        column = lax.rem(my_part + lax.rem(step, stretch), stretch)
-        side = lax.rem(my_place // half + lax.rem(k, halves), halves)
-        return column * ctx + side * half + lax.rem(lax.rem(my_place, half) + step // stretch, half)
+        return lax.rem(me + k * stride, n)
 
     def place(device):
         return (device // ctx, lax.rem(device, ctx))
@@ -150,19 +146,14 @@
             weight = jnp.where(block - lag >= start, 1.0, 0.0).astype(jnp.float32)
             live[block, lag] = jnp.full(live.shape[2:], weight, jnp.float32).astype(jnp.bfloat16)
 
-    if chunks > 1:
-
-        @pl.loop(1, n)
-        def _(k):
-            copy_in(1, peer(k), me).start()
+    for chunk in range(1, chunks):
+
+        @pl.loop(1, n)
+        def _(k, chunk=chunk):
+            copy_in(chunk - 1, peer(k), me).wait_send()
+            copy_in(chunk, peer(k), me).start()
 
     for chunk in range(chunks):
-
-        @pl.loop(1, n)
-        def _(k, chunk=chunk):
-            if chunk == 0 and chunks > 2:
-                copy_in(0, peer(k), me).wait_send()
-                copy_in(2, peer(k), me).start()
 
         @pl.loop(1, n)
         def _(k, chunk=chunk):
@@ -194,15 +185,10 @@
 
         back[chunk, me] = mixed[chunk, me]
 
-        for later in range(3, chunks) if chunk == 0 else ():
-
-            @pl.loop(1, n)
-            def _(k, later=later):
-                copy_in(later - 2, peer(k), me).wait_send()
-                copy_in(later, peer(k), me).start()
-
-        @pl.loop(1, n)
-        def _(k, chunk=chunk):
+        @pl.loop(1, n)
+        def _(k, chunk=chunk):
+            if chunk == 0:
+                copy_in(chunks - 1, peer(k), me).wait_send()
             copy_back(chunk, peer(k), me).start()
 
     def finish(lanes, turned):
@@ -241,8 +227,6 @@
 
         @pl.loop(1, n)
         def _(k, chunk=chunk):
-            if chunk + 2 >= chunks:
-                copy_in(chunk, peer(k), me).wait_send()
             copy_back(chunk, peer(k), me).wait_send()
 
 
@@ -256,7 +240,7 @@
     blocks = n * tok_rows // BLK
     longest = blocks * 3 // 8
     lags = min(longest, taps // BLK + 1)
-    chunks = share // (2 * width) if share % BLK == 0 else 1
+    chunks = share // BLK if share % BLK == 0 else 1
     rows = share // chunks
     slab = (chunks, n, rows, BLK)
     vmem = pl.BlockSpec(memory_space=pltpu.VMEM)

time: 115 us -> 111 us (0.965)
  Pallas kernels: 111 us -> 107 us
    pallas_call x1, Pallas kernels: 111 us -> 107 us  [per_device(): pl.pallas_call(functools.partial(kernel, stretch, ctx, chunks, lags, widt...]
where the time goes in v4:
time: 111 us
  Pallas kernels  107 us (96%)
  other arithmetic  3.41 us (3%)
    pallas_call x1, Pallas kernels, per_device(): pl.pallas_call(functools.partial(kernel, stretch, ctx, chunks, lags, widt...  107 us
    convert_element_type x1, other arithmetic, per_device(): (post_gate.astype(jnp.float32) * returned.astype(jnp.float32)).astype(jnp...  3.41 us

profile of v4, /device:TPU:0, one launch (start us, length us, event | category | flops | bytes accessed | tf_op | source)
XLA Modules:
  0.0 110.6 jit_solution(12137677888760287161)
XLA Ops:
  0.0 0.0 copy-start
  0.0 107.2 %shard_map.64 = bf16[128,8192]{1,0:T(8,128)(2,1)} custom-call(bf16[128,8192]{1,0:T(8,128)(2,1)} %pre_ref.1, bf16[128,8192]{1,0:T(8,128)(2,1)} %val_ref.1, f32[32,4096]{1,0:T(8,128)} %filt_ref.1, f32[1024]{0:T(1024)} %skip_ref.1, s32[16]{0:T(128)} %docs_ref.1), custom_call_target="tpu_custom_call" | custom-call | tf_op jit(solution)/shard_map/pallas_call | solution.py:248
  107.2 0.0 copy-done
  107.2 3.4 %multiply_convert_fusion = bf16[128,8192]{1,0:T(8,128)(2,1)} fusion(bf16[128,8192]{1,0:T(8,128)(2,1)} %shard_map.64, bf16[128,8192]{1,0:T(8,128)(2,1)S(1)} %copy-done), kind=kLoop, calls=%fused_computation | loop fusion | flops 4194304 | bytes 6291456 | tf_op jit(solution)/shard_map/convert_element_type | solution.py:277
Async XLA Ops:
  0.0 107.2 %copy-start = (bf16[128,8192]{1,0:T(8,128)(2,1)S(1)}, bf16[128,8192]{1,0:T(8,128)(2,1)}, u32[]{:S(2)}) copy-start(bf16[128,8192]{1,0:T(8,128)(2,1)} %param.6) | copy-start | bytes 6291460

commit v5 on v4

--- a/solution.py
+++ b/solution.py
@@ -10,6 +10,7 @@
 
 BLK = 128
 TILE_BLOCKS = 8
+GATE_STEPS = 4
 MESH = pl.DeviceIdType.MESH
 
 
@@ -17,15 +18,10 @@
     stretch, ctx, chunks, lags, width,
     pre_ref, val_ref, filt_ref, skip_ref, docs_ref, out_ref,
     pre, val, filt, gated, arrived, mixed, back, toeplitz, skips, live,
-    load_sem, send_in, recv_in, send_back, recv_back,
+    load_sem, pre_sem, val_sem, send_in, recv_in, send_back, recv_back,
 ):
-    loads = [
-        pltpu.make_async_copy(pre_ref, pre, load_sem.at[0]),
-        pltpu.make_async_copy(val_ref, val, load_sem.at[1]),
-        pltpu.make_async_copy(filt_ref, filt, load_sem.at[2]),
-    ]
-    for load in loads:
-        load.start()
+    filter_load = pltpu.make_async_copy(filt_ref, filt, load_sem)
+    filter_load.start()
     part = lax.axis_index("stretch")
     n = stretch * ctx
     me = lax.axis_index("stretch") * ctx + lax.axis_index("ctx")
@@ -44,11 +40,37 @@
     def slab_of(device):
         return lax.rem(device, ctx) * stretch + device // ctx
 
+    unit = max(share, BLK)
+    per_unit = unit // share
+
+    tiles = n // per_unit
+
+    def tile_at(turn):
+        return slab_of(peer(turn)) if per_unit == 1 else turn
+
+    def tile_loads(turn):
+        lanes = pl.ds(pl.multiple_of(tile_at(turn) * unit, unit), unit)
+        return (
+            pltpu.make_async_copy(pre_ref.at[:, lanes], pre.at[:, lanes], pre_sem.at[turn]),
+            pltpu.make_async_copy(val_ref.at[:, lanes], val.at[:, lanes], val_sem.at[turn]),
+        )
+
+    early = n // 8 if per_unit == 1 else n
     barrier = pltpu.get_barrier_semaphore()
+
+    @pl.loop(0, min(early, tiles))
+    def _(turn):
+        for load in tile_loads(turn):
+            load.start()
 
     @pl.loop(1, n)
     def _(k):
         pl.semaphore_signal(barrier, inc=1, device_id=place(peer(k)), device_id_type=MESH)
+
+    @pl.loop(min(early, tiles), tiles)
+    def _(turn):
+        for load in tile_loads(turn):
+            load.start()
 
     def copy_in(chunk, device, slot):
         return pltpu.make_async_remote_copy(
@@ -70,10 +92,10 @@
             device_id_type=MESH,
         )
 
-    unit = max(share, BLK)
-    per_unit = unit // share
-
-    def gate(tile):
+    def gate(turn):
+        for load in tile_loads(turn):
+            load.wait()
+        tile = tile_at(turn)
         lanes = pl.ds(pl.multiple_of(tile * unit, unit), unit)
         product = pre[:, lanes].astype(jnp.float32) * val[:, lanes].astype(jnp.float32)
         turned = product.T.astype(jnp.bfloat16)
@@ -82,21 +104,9 @@
                 first = slab * share + chunk * rows
                 gated[chunk, tile * per_unit + slab] = turned[first : first + rows]
 
-    for load in loads[:2]:
-        load.wait()
-    early = n // 4 if per_unit == 1 else n
-
-    if per_unit == 1:
-
-        @pl.loop(0, early)
-        def _(k):
-            gate(slab_of(peer(k)))
-
-    else:
-
-        @pl.loop(0, n // per_unit)
-        def _(tile):
-            gate(tile)
+    @pl.loop(0, min(early, tiles))
+    def _(turn):
+        gate(turn)
 
     pl.semaphore_wait(barrier, n - 1)
 
@@ -106,14 +116,14 @@
 
     @pl.loop(early, n)
     def _(k):
-        gate(slab_of(peer(k)))
+        gate(k)
         copy_in(0, peer(k), me).start()
 
     for chunk in range(chunks):
         arrived[chunk, lead + me] = gated[chunk, slab_of(me)]
         arrived[chunk, 0:lead] = jnp.zeros((lead, rows, BLK), jnp.bfloat16)
 
-    loads[2].wait()
+    filter_load.wait()
     taps = filt.shape[1]
 
     @pl.loop(0, chunks * chunk_groups)
@@ -228,6 +238,11 @@
         @pl.loop(1, n)
         def _(k, chunk=chunk):
             copy_back(chunk, peer(k), me).wait_send()
+
+
+def gate_kernel(post_ref, mixed_ref, out_ref):
+    product = post_ref[...].astype(jnp.float32) * mixed_ref[...].astype(jnp.float32)
+    out_ref[...] = product.astype(jnp.bfloat16)
 
 
 def per_device(stretch, ctx, post_gate, pre_gate, values, filters, skip_bias, doc_blocks):
@@ -267,14 +282,24 @@
             pltpu.VMEM((groups, lags * BLK, BLK), jnp.bfloat16),
             pltpu.VMEM((stretch * share, BLK), jnp.float32),
             pltpu.VMEM((blocks, lags, 16, BLK), jnp.bfloat16),
-            pltpu.SemaphoreType.DMA((3,)),
+            pltpu.SemaphoreType.DMA(()),
+            pltpu.SemaphoreType.DMA((n,)),
+            pltpu.SemaphoreType.DMA((n,)),
             sems, sems, sems, sems,
         ],
         compiler_params=pltpu.CompilerParams(
             collective_id=0, has_side_effects=True, vmem_limit_bytes=58 * 1024 * 1024
         ),
     )(pre_gate, values, filters, skip_bias, doc_blocks)
-    return (post_gate.astype(jnp.float32) * returned.astype(jnp.float32)).astype(jnp.bfloat16)
+    block = pl.BlockSpec((tok_rows // GATE_STEPS, model), lambda step: (step, 0))
+    return pl.pallas_call(
+        gate_kernel,
+        out_shape=jax.ShapeDtypeStruct((tok_rows, model), jnp.bfloat16),
+        grid=(GATE_STEPS,),
+        in_specs=[block, block],
+        out_specs=block,
+        compiler_params=pltpu.CompilerParams(vmem_limit_bytes=58 * 1024 * 1024),
+    )(post_gate, returned)
 
 
 def solution(mesh):

time: 111 us -> 112 us (level)
  Pallas kernels: 107 us -> 112 us
  other arithmetic: 3.41 us -> 0 us
    pallas_call x0 -> x1, Pallas kernels: none -> 4.31 us  [per_device(): pl.pallas_call(gate_kernel, out_shape=jax.ShapeDtypeStruct((tok_rows, mod...]
    convert_element_type x1 -> x0, other arithmetic: 3.41 us -> none  [per_device(): (post_gate.astype(jnp.float32) * returned.astype(jnp.float32)).astype(jnp...]
where the time goes in v5:
time: 112 us
  Pallas kernels  112 us (100%)
    pallas_call x1, Pallas kernels, per_device(): pl.pallas_call(functools.partial(kernel, stretch, ctx, chunks, lags, widt...  108 us
    pallas_call x1, Pallas kernels, per_device(): pl.pallas_call(gate_kernel, out_shape=jax.ShapeDtypeStruct((tok_rows, mod...  4.31 us

profile of v5, /device:TPU:0, one launch (start us, length us, event | category | flops | bytes accessed | tf_op | source)
XLA Modules:
  0.0 112.0 jit_solution(7576085192068953884)
XLA Ops:
  0.0 107.7 %shard_map.64.mixed_ref = bf16[128,8192]{1,0:T(8,128)(2,1)} custom-call(bf16[128,8192]{1,0:T(8,128)(2,1)} %pre_ref.1, bf16[128,8192]{1,0:T(8,128)(2,1)} %val_ref.1, f32[32,4096]{1,0:T(8,128)} %filt_ref.1, f32[1024]{0:T(1024)} %skip_ref.1, s32[16]{0:T(128)} %docs_ref.1), custom_call_target="tpu_custom_call" | custom-call | tf_op jit(solution)/shard_map/pallas_call | solution.py:263
  107.7 4.3 %shard_map.65 = bf16[128,8192]{1,0:T(8,128)(2,1)} custom-call(bf16[128,8192]{1,0:T(8,128)(2,1)} %post_ref.1, bf16[128,8192]{1,0:T(8,128)(2,1)} %shard_map.64.mixed_ref), custom_call_target="tpu_custom_call" | custom-call | tf_op jit(solution)/shard_map/pallas_call | solution.py:295

commit v6 on v4

--- a/solution.py
+++ b/solution.py
@@ -109,6 +109,12 @@
         gate(slab_of(peer(k)))
         copy_in(0, peer(k), me).start()
 
+    for chunk in range(1, chunks):
+
+        @pl.loop(1, n)
+        def _(k, chunk=chunk):
+            copy_in(chunk, peer(k), me).start()
+
     for chunk in range(chunks):
         arrived[chunk, lead + me] = gated[chunk, slab_of(me)]
         arrived[chunk, 0:lead] = jnp.zeros((lead, rows, BLK), jnp.bfloat16)
@@ -145,13 +151,6 @@
         for lag in range(lags):
             weight = jnp.where(block - lag >= start, 1.0, 0.0).astype(jnp.float32)
             live[block, lag] = jnp.full(live.shape[2:], weight, jnp.float32).astype(jnp.bfloat16)
-
-    for chunk in range(1, chunks):
-
-        @pl.loop(1, n)
-        def _(k, chunk=chunk):
-            copy_in(chunk - 1, peer(k), me).wait_send()
-            copy_in(chunk, peer(k), me).start()
 
     for chunk in range(chunks):
 
@@ -187,8 +186,6 @@
 
         @pl.loop(1, n)
         def _(k, chunk=chunk):
-            if chunk == 0:
-                copy_in(chunks - 1, peer(k), me).wait_send()
             copy_back(chunk, peer(k), me).start()
 
     def finish(lanes, turned):
@@ -227,6 +224,7 @@
 
         @pl.loop(1, n)
         def _(k, chunk=chunk):
+            copy_in(chunk, peer(k), me).wait_send()
             copy_back(chunk, peer(k), me).wait_send()
 
 

time: 111 us -> 111 us (level)
  no operation moved by 1% of the time
where the time goes in v6:
time: 111 us
  Pallas kernels  107 us (96%)
  other arithmetic  3.41 us (3%)
    pallas_call x1, Pallas kernels, per_device(): pl.pallas_call(functools.partial(kernel, stretch, ctx, chunks, lags, widt...  107 us
    convert_element_type x1, other arithmetic, per_device(): (post_gate.astype(jnp.float32) * returned.astype(jnp.float32)).astype(jnp...  3.41 us

profile of v6, /device:TPU:0, one launch (start us, length us, event | category | flops | bytes accessed | tf_op | source)
XLA Modules:
  0.0 110.7 jit_solution(3528288863446182680)
XLA Ops:
  0.0 0.0 copy-start
  0.0 107.3 %shard_map.64 = bf16[128,8192]{1,0:T(8,128)(2,1)} custom-call(bf16[128,8192]{1,0:T(8,128)(2,1)} %pre_ref.1, bf16[128,8192]{1,0:T(8,128)(2,1)} %val_ref.1, f32[32,4096]{1,0:T(8,128)} %filt_ref.1, f32[1024]{0:T(1024)} %skip_ref.1, s32[16]{0:T(128)} %docs_ref.1), custom_call_target="tpu_custom_call" | custom-call | tf_op jit(solution)/shard_map/pallas_call | solution.py:246
  107.3 0.0 copy-done
  107.3 3.4 %multiply_convert_fusion = bf16[128,8192]{1,0:T(8,128)(2,1)} fusion(bf16[128,8192]{1,0:T(8,128)(2,1)} %shard_map.64, bf16[128,8192]{1,0:T(8,128)(2,1)S(1)} %copy-done), kind=kLoop, calls=%fused_computation | loop fusion | flops 4194304 | bytes 6291456 | tf_op jit(solution)/shard_map/convert_element_type | solution.py:275
Async XLA Ops:
  0.0 107.3 %copy-start = (bf16[128,8192]{1,0:T(8,128)(2,1)S(1)}, bf16[128,8192]{1,0:T(8,128)(2,1)}, u32[]{:S(2)}) copy-start(bf16[128,8192]{1,0:T(8,128)(2,1)} %param.6) | copy-start | bytes 6291460

commit v7 on v6

--- a/solution.py
+++ b/solution.py
@@ -15,14 +15,15 @@
 
 def kernel(
     stretch, ctx, chunks, lags, width,
-    pre_ref, val_ref, filt_ref, skip_ref, docs_ref, out_ref,
-    pre, val, filt, gated, arrived, mixed, back, toeplitz, skips, live,
+    pre_ref, val_ref, post_ref, filt_ref, skip_ref, docs_ref, out_ref,
+    pre, val, post, filt, gated, arrived, mixed, back, toeplitz, skips, live,
     load_sem, send_in, recv_in, send_back, recv_back,
 ):
     loads = [
         pltpu.make_async_copy(pre_ref, pre, load_sem.at[0]),
         pltpu.make_async_copy(val_ref, val, load_sem.at[1]),
         pltpu.make_async_copy(filt_ref, filt, load_sem.at[2]),
+        pltpu.make_async_copy(post_ref, post, load_sem.at[3]),
     ]
     for load in loads:
         load.start()
@@ -120,6 +121,7 @@
         arrived[chunk, 0:lead] = jnp.zeros((lead, rows, BLK), jnp.bfloat16)
 
     loads[2].wait()
+    loads[3].wait()
     taps = filt.shape[1]
 
     @pl.loop(0, chunks * chunk_groups)
@@ -189,7 +191,8 @@
             copy_back(chunk, peer(k), me).start()
 
     def finish(lanes, turned):
-        out_ref[:, lanes] = turned.astype(jnp.float32).T.astype(jnp.bfloat16)
+        product = turned.astype(jnp.float32).T * post[:, lanes].astype(jnp.float32)
+        out_ref[:, lanes] = product.astype(jnp.bfloat16)
 
     joint = max(BLK // rows, 1)
     if share % BLK == 0:
@@ -243,10 +246,11 @@
     slab = (chunks, n, rows, BLK)
     vmem = pl.BlockSpec(memory_space=pltpu.VMEM)
     sems = pltpu.SemaphoreType.DMA((chunks, n))
-    returned = pl.pallas_call(
+    return pl.pallas_call(
         functools.partial(kernel, stretch, ctx, chunks, lags, width),
         out_shape=jax.ShapeDtypeStruct((tok_rows, model), jnp.bfloat16),
         in_specs=[
+            pl.BlockSpec(memory_space=pltpu.HBM),
             pl.BlockSpec(memory_space=pltpu.HBM),
             pl.BlockSpec(memory_space=pltpu.HBM),
             pl.BlockSpec(memory_space=pltpu.HBM),
@@ -255,6 +259,7 @@
         ],
         out_specs=vmem,
         scratch_shapes=[
+            pltpu.VMEM((tok_rows, model), jnp.bfloat16),
             pltpu.VMEM((tok_rows, model), jnp.bfloat16),
             pltpu.VMEM((tok_rows, model), jnp.bfloat16),
             pltpu.VMEM(filters.shape, jnp.float32),
@@ -265,14 +270,13 @@
             pltpu.VMEM((groups, lags * BLK, BLK), jnp.bfloat16),
             pltpu.VMEM((stretch * share, BLK), jnp.float32),
             pltpu.VMEM((blocks, lags, 16, BLK), jnp.bfloat16),
-            pltpu.SemaphoreType.DMA((3,)),
+            pltpu.SemaphoreType.DMA((4,)),
             sems, sems, sems, sems,
         ],
         compiler_params=pltpu.CompilerParams(
-            collective_id=0, has_side_effects=True, vmem_limit_bytes=58 * 1024 * 1024
+            collective_id=0, has_side_effects=True, vmem_limit_bytes=51 * 1024 * 1024
         ),
-    )(pre_gate, values, filters, skip_bias, doc_blocks)
-    return (post_gate.astype(jnp.float32) * returned.astype(jnp.float32)).astype(jnp.bfloat16)
+    )(pre_gate, values, post_gate, filters, skip_bias, doc_blocks)
 
 
 def solution(mesh):

time: 111 us -> 110 us (level)
  local copies, waits for them, and re-layouts: 0.01 us -> 3.7 us
  other arithmetic: 3.41 us -> 0 us
    unnamed x2 -> x7, local copies, waits for them, and re-layouts: 0.01 us -> 3.7 us
    convert_element_type x1 -> x0, other arithmetic: 3.41 us -> none  [per_device(): (post_gate.astype(jnp.float32) * returned.astype(jnp.float32)).astype(jnp...]
    pallas_call x1, Pallas kernels: 107 us -> 106 us  [per_device(): pl.pallas_call(functools.partial(kernel, stretch, ctx, chunks, lags, widt...]
where the time goes in v7:
time: 110 us; the launch traced here: 109 us
  Pallas kernels  106 us (96%)
  local copies, waits for them, and re-layouts  3.7 us (3%)
    pallas_call x1, Pallas kernels, per_device(): pl.pallas_call(functools.partial(kernel, stretch, ctx, chunks, lags, widt...  106 us
    unnamed x7, local copies, waits for them, and re-layouts  3.7 us

profile of v7, /device:TPU:0, one launch (start us, length us, event | category | flops | bytes accessed | tf_op | source)
XLA Modules:
  0.0 109.4 jit_solution(2392352123932627557)
XLA Ops:
  0.0 0.0 copy-start
  0.0 1.0 copy-done
  1.0 0.0 copy-start.1
  1.0 0.7 copy-done.1
  1.7 0.0 copy-start.2
  1.7 0.7 copy-done.2
  2.4 105.7 %shard_map.64 = bf16[128,8192]{1,0:T(8,128)(2,1)S(1)} custom-call(bf16[128,8192]{1,0:T(8,128)(2,1)} %pre_ref.1, bf16[128,8192]{1,0:T(8,128)(2,1)} %val_ref.1, bf16[128,8192]{1,0:T(8,128)(2,1)} %post_ref.1, f32[32,4096]{1,0:T(8,128)S(1)} %copy-done, f32[1024]{0:T(1024)S(1)} %copy-done.1, s32[16]{0:T(128)S(1)} %copy-done.2), custom_call_target="tpu_custom_call" | custom-call | tf_op jit(solution)/shard_map/pallas_call | solution.py:249
  108.1 1.3 %copy.8 = bf16[128,8192]{1,0:T(8,128)(2,1)} copy(bf16[128,8192]{1,0:T(8,128)(2,1)S(1)} %shard_map.64) | data formatting | bytes 4194304
Async XLA Ops:
  0.0 1.0 copy-start
  1.0 0.7 copy-start.1
  1.7 0.7 copy-start.2

commit v8 on v7

--- a/solution.py
+++ b/solution.py
@@ -34,7 +34,7 @@
     share = chunks * rows
     lead = lags - 1
     chunk_groups = rows // width
-    stride = 5 if math.gcd(5, n) == 1 else 1
+    stride = 3 if math.gcd(3, n) == 1 else 1
 
     def peer(k):
         return lax.rem(me + k * stride, n)

time: 110 us -> 109 us (level)
  no operation moved by 1% of the time
where the time goes in v8:
time: 109 us; the launch traced here: 108 us
  Pallas kernels  105 us (96%)
  local copies, waits for them, and re-layouts  3.7 us (3%)
    pallas_call x1, Pallas kernels, per_device(): pl.pallas_call(functools.partial(kernel, stretch, ctx, chunks, lags, widt...  105 us
    unnamed x7, local copies, waits for them, and re-layouts  3.7 us

profile of v8, /device:TPU:0, one launch (start us, length us, event | category | flops | bytes accessed | tf_op | source)
XLA Modules:
  0.0 108.3 jit_solution(11936624297493670560)
XLA Ops:
  0.0 0.0 copy-start
  0.0 1.0 copy-done
  1.0 0.0 copy-start.1
  1.0 0.7 copy-done.1
  1.7 0.0 copy-start.2
  1.7 0.7 copy-done.2
  2.4 104.6 %shard_map.64 = bf16[128,8192]{1,0:T(8,128)(2,1)S(1)} custom-call(bf16[128,8192]{1,0:T(8,128)(2,1)} %pre_ref.1, bf16[128,8192]{1,0:T(8,128)(2,1)} %val_ref.1, bf16[128,8192]{1,0:T(8,128)(2,1)} %post_ref.1, f32[32,4096]{1,0:T(8,128)S(1)} %copy-done, f32[1024]{0:T(1024)S(1)} %copy-done.1, s32[16]{0:T(128)S(1)} %copy-done.2), custom_call_target="tpu_custom_call" | custom-call | tf_op jit(solution)/shard_map/pallas_call | solution.py:249
  107.0 1.3 %copy.8 = bf16[128,8192]{1,0:T(8,128)(2,1)} copy(bf16[128,8192]{1,0:T(8,128)(2,1)S(1)} %shard_map.64) | data formatting | bytes 4194304
Async XLA Ops:
  0.0 1.0 copy-start
  1.0 0.7 copy-start.1
  1.7 0.7 copy-start.2
